TPU v7x, 512 devices: a whole 4x8x8 slice. The times are simulated.
512 devices in a mesh: stratum: 128 (over y, z_lo, x), rep: 4 (over z_hi, core).
Axes of the slice: x: 4, y: 8, z: 8 (z_hi: 2, z_lo: 4; z = z_hi * 4 + z_lo), core: 2. Of those that a mesh axis runs over, the one named last changes fastest.
Arguments:
- user_rows: float32 [524288, 256], P(('stratum', 'rep')), may hold values from -1.5 to 1.5
- user_accum: float32 [524288], P(('stratum', 'rep')), may hold values from 4 to 400
- item_rows: float32 [65536, 256], P('stratum'), may hold values from -1.5 to 1.5
- item_accum: float32 [65536, 256], P('stratum'), may hold values from 30 to 3000
- move_lists: int32 [3, 128], replicated, may hold values from 0 to 127, each once within a row
- tile_lists: int32 [3, 128, 4, 32], P(None, 'stratum', 'rep'), may hold values from 0 to 31, each once within a row
- tile_counts: int32 [3, 128, 4], P(None, 'stratum', 'rep'), may hold values from 4 to 32, as said below
- rating_bits: int32 [3, 128, 4, 32, 16, 128], P(None, 'stratum', 'rep'), may hold values from 0 to 255
Outputs:
- new_users: float32 [524288, 256], P(('stratum', 'rep'))
- new_items: float32 [65536, 256], P('stratum')
Inputs may be any that keep to these rules, and one draw needn't show every extreme that they name: `move_lists`: each row is a permutation of the 128 block positions. `tile_lists`: each list is a permutation of the 32 slots; only its first tile_counts entries are used. `tile_counts`: in every stratum some pair uses all 32 slots.
All inputs are finite; a program needn't handle non-finite values.
Results may differ from a plain program's by a relative error of at most 0.011.
Values may be sent and summed in bfloat16 or wider, within the bound.
A program may use at most 64 MiB of HBM per device.

v0:
```python
import jax
import jax.numpy as jnp
from jax import lax
from jax.sharding import PartitionSpec as P

STRATA = 3


CONFIDENCE = 2.0
SHRINKAGE = 0.02
RATE_START = 0.25
RATE_DECAY = 0.75


def unpack_bits(bit_words):
    shifts = jnp.arange(8, dtype=jnp.int32)
    bit_flags = jnp.bitwise_and(
        jnp.right_shift(bit_words[:, :, None, :], shifts[None, None, :, None]), 1
    )
    return bit_flags.reshape(bit_words.shape[0], bit_words.shape[1] * 8, bit_words.shape[2]).astype(
        jnp.float32
    )


def invert(targets):
    entries = targets.shape[0]
    numbers = jnp.arange(entries, dtype=jnp.int32)
    return jnp.sum(jnp.where(targets[None, :] == numbers[:, None], numbers[None, :], 0), axis=1)


def rep_total(item_part):
    return lax.psum(item_part, "rep")


def tile_terms(user_state, item_low, tile_list, tile_count, bit_words, col_tiles):
    tile_size = bit_words.shape[-1]
    width = user_state.shape[1]
    row_tiles = user_state.shape[0] // tile_size
    user_tiles = user_state.astype(jnp.bfloat16).reshape(row_tiles, tile_size, width)
    item_tiles = item_low.reshape(col_tiles, tile_size, width)
    slot_total = tile_list.shape[0]
    batch_tiles = 8
    row_numbers = jnp.arange(row_tiles, dtype=jnp.int32)
    col_numbers = jnp.arange(col_tiles, dtype=jnp.int32)

    def one_group(group_idx, carry):
        user_sum, item_sum = carry
        position = group_idx * batch_tiles + jnp.arange(batch_tiles, dtype=jnp.int32)
        active = (position < tile_count).astype(jnp.float32)
        clamped = jnp.minimum(position, slot_total - 1)
        slot_ids = jnp.take(tile_list, clamped)
        row_ids = slot_ids // col_tiles
        col_ids = slot_ids % col_tiles
        user_pick = jnp.take(user_tiles, row_ids, axis=0)
        item_pick = jnp.take(item_tiles, col_ids, axis=0)
        observed = unpack_bits(jnp.take(bit_words, clamped, axis=0))
        scores = jnp.einsum(
            "gur,gir->giu", user_pick, item_pick, preferred_element_type=jnp.float32
        )
        residual = (
            active[:, None, None] * (1.0 + CONFIDENCE * observed) * (scores - observed)
        ).astype(jnp.bfloat16)
        user_part = jnp.einsum(
            "giu,gir->gur", residual, item_pick, preferred_element_type=jnp.float32
        )
        item_part = jnp.einsum(
            "giu,gur->gir", residual, user_pick, preferred_element_type=jnp.float32
        )
        row_hot = (row_ids[:, None] == row_numbers[None, :]).astype(jnp.float32)
        col_hot = (col_ids[:, None] == col_numbers[None, :]).astype(jnp.float32)
        user_sum = user_sum + jnp.einsum(
            "ga,gur->aur", row_hot, user_part, precision=lax.Precision.HIGHEST
        )
        item_sum = item_sum + jnp.einsum(
            "gc,gir->cir", col_hot, item_part, precision=lax.Precision.HIGHEST
        )
        return (user_sum, item_sum)

    initial = (
        jnp.zeros((row_tiles, tile_size, width), jnp.float32),
        jnp.zeros((col_tiles, tile_size, width), jnp.float32),
    )
    groups = (tile_count + batch_tiles - 1) // batch_tiles
    user_sum, item_sum = lax.fori_loop(0, groups, one_group, initial)
    user_grad = user_sum.reshape(-1, width) + SHRINKAGE * user_state
    return (user_grad, item_sum.reshape(-1, width))


def adagrad_rows(user_state, user_acc, user_grad, step_rate):
    acc_next = user_acc + jnp.mean(user_grad * user_grad, axis=1)
    return (user_state - step_rate * user_grad / jnp.sqrt(acc_next)[:, None], acc_next)


def on_device(
    user_rows, user_accum, item_rows, item_accum, move_lists, tile_lists, tile_counts, rating_bits
):
    blocks = lax.axis_size("stratum")
    width = item_rows.shape[1]
    block_rows = item_rows.shape[0]
    piece_rows = block_rows // blocks
    col_tiles = block_rows // rating_bits.shape[-1]
    user_state = user_rows
    user_acc = user_accum
    item_state = jnp.stack([item_rows, item_accum])
    for stratum_idx in range(STRATA):
        step_rate = RATE_START * RATE_DECAY**stratum_idx
        sources = invert(move_lists[stratum_idx])
        pieces = item_state.reshape(2, blocks, piece_rows, width)
        spread = lax.all_to_all(pieces, "stratum", split_axis=1, concat_axis=1, tiled=True)
        ordered = jnp.take(spread, sources, axis=1)
        item_state = lax.all_to_all(
            ordered, "stratum", split_axis=1, concat_axis=1, tiled=True
        ).reshape(2, block_rows, width)
        item_low = item_state[0].astype(jnp.bfloat16)
        user_grad, item_part = tile_terms(
            user_state,
            item_low,
            tile_lists[stratum_idx, 0, 0],
            tile_counts[stratum_idx, 0, 0],
            rating_bits[stratum_idx, 0, 0],
            col_tiles,
        )
        user_state, user_acc = adagrad_rows(user_state, user_acc, user_grad, step_rate)
        item_grad = rep_total(item_part) + SHRINKAGE * item_state[0]
        acc_next = item_state[1] + item_grad * item_grad
        item_state = jnp.stack(
            [item_state[0] - step_rate * item_grad / jnp.sqrt(acc_next), acc_next]
        )
    item_out = item_state[0]
    return (user_state, item_out)


def solution(mesh):
    in_specs = (
        P(("stratum", "rep"), None),
        P(("stratum", "rep")),
        P("stratum", None),
        P("stratum", None),
        P(),
        P(None, "stratum", "rep", None),
        P(None, "stratum", "rep"),
        P(None, "stratum", "rep", None, None, None),
    )
    out_specs = (P(("stratum", "rep"), None), P("stratum", None))
    return jax.shard_map(
        on_device, mesh=mesh, in_specs=in_specs, out_specs=out_specs, check_vma=False
    )
```

profile of v0, /device:TPU:1, one launch (start us, length us, event | category | flops | bytes accessed | tf_op | source)
XLA Modules:
  0.0 554.9 jit_solution(13452417550215738833)
XLA Ops:
  7.2 1.2 stack.27
  8.6 1.2 pad_maximum_fusion
  9.8 17.9 %all-to-all-start = ((f32[2,128,4,256]{3,2,0,1:T(4,128)}), f32[2,128,4,256]{3,2,0,1:T(4,128)S(1)}, u32[]{:S(2)}, u32[]{:S(2)}) async-start(f32[2,128,4,256]{3,2,0,1:T(4,128)} %pad_maximum_fusion), calls=%async_computation | async-start | bytes 2097152 | tf_op jit(solution)/shard_map/all_to_all | solution.py:109
  27.9 27.8 %all-to-all-done = f32[2,128,4,256]{3,2,0,1:T(4,128)S(1)} async-done(((f32[2,128,4,256]{3,2,0,1:T(4,128)}), f32[2,128,4,256]{3,2,0,1:T(4,128)S(1)}, u32[]{:S(2)}, u32[]{:S(2)}) %all-to-all-start) | async-done | bytes 1048608 | tf_op jit(solution)/shard_map/all_to_all | solution.py:109
  55.9 1.2 gather_fusion.12
  57.1 1.3 select_bitcast_fusion.2
  58.4 8.6 %all-to-all-start.1 = ((f32[2,128,4,256]{3,2,0,1:T(4,128)}), f32[2,128,4,256]{3,2,0,1:T(4,128)S(1)}, u32[]{:S(2)}, u32[]{:S(2)}) async-start(f32[2,128,4,256]{3,2,0,1:T(4,128)} %select_bitcast_fusion.2), calls=%async_computation.1 | async-start | bytes 2097152 | tf_op jit(solution)/shard_map/all_to_all | solution.py:111
  70.4 23.8 %all-to-all-done.1 = f32[2,128,4,256]{3,2,0,1:T(4,128)S(1)} async-done(((f32[2,128,4,256]{3,2,0,1:T(4,128)}), f32[2,128,4,256]{3,2,0,1:T(4,128)S(1)}, u32[]{:S(2)}, u32[]{:S(2)}) %all-to-all-start.1) | async-done | bytes 1048608 | tf_op jit(solution)/shard_map/all_to_all | solution.py:111
  95.3 14.7 %while.45 = (s32[]{:T(128)}, f32[8,128,256]{2,0,1:T(8,128)S(1)}, f32[4,128,256]{2,0,1:T(4,128)S(1)}, s32[]{:T(128)}, s32[32]{0:T(128)S(1)}, /*index=5*/s32[]{:T(...) while((s32[]{:T(128)}, f32[8,128,256]{2,0,1:T(8,128)S(1)}, ...), condition=%wide.region_2.8_spmd.clone, body=%wide.region_1.7_spmd.clone.sunk | while | flops 241716768 | bytes 14760929 | solution.py:84
  99.5 1.4 convolution_add_fusion.13
  101.3 1.3 convolution_add_fusion.12
  106.9 1.4 convolution_add_fusion.13
  108.7 1.3 convolution_add_fusion.12
  112.0 79.4 %all-reduce.4.cloned.1.call-done = f32[512,256]{1,0:T(8,128)} async-done(((f32[512,256]{1,0:T(8,128)}), f32[512,256]{1,0:T(8,128)}) %all-reduce.4.cloned.1.call-update) | async-done | bytes 524304 | tf_op jit(solution)/shard_map/psum | solution.py:32
  191.4 1.2 multiply_subtract_fusion.2
  193.0 1.2 pad_maximum_fusion.1
  194.2 12.1 %all-to-all-start.2 = ((f32[2,128,4,256]{3,2,0,1:T(4,128)}), f32[2,128,4,256]{3,2,0,1:T(4,128)S(1)}, u32[]{:S(2)}, u32[]{:S(2)}) async-start(f32[2,128,4,256]{3,2,0,1:T(4,128)} %pad_maximum_fusion.1), calls=%async_computation.2 | async-start | bytes 2097152 | tf_op jit(solution)/shard_map/all_to_all | solution.py:109
  206.4 28.4 %all-to-all-done.2 = f32[2,128,4,256]{3,2,0,1:T(4,128)S(1)} async-done(((f32[2,128,4,256]{3,2,0,1:T(4,128)}), f32[2,128,4,256]{3,2,0,1:T(4,128)S(1)}, u32[]{:S(2)}, u32[]{:S(2)}) %all-to-all-start.2) | async-done | bytes 1048608 | tf_op jit(solution)/shard_map/all_to_all | solution.py:109
  235.0 1.2 gather_fusion.13
  236.2 1.3 select_bitcast_fusion.1
  237.5 8.5 %all-to-all-start.3 = ((f32[2,128,4,256]{3,2,0,1:T(4,128)}), f32[2,128,4,256]{3,2,0,1:T(4,128)}, u32[]{:S(2)}, u32[]{:S(2)}) async-start(f32[2,128,4,256]{3,2,0,1:T(4,128)} %select_bitcast_fusion.1), calls=%async_computation.3 | async-start | bytes 2097152 | tf_op jit(solution)/shard_map/all_to_all | solution.py:111
  248.6 1.3 fusion.75
  249.9 22.6 %all-to-all-done.3 = f32[2,128,4,256]{3,2,0,1:T(4,128)} async-done(((f32[2,128,4,256]{3,2,0,1:T(4,128)}), f32[2,128,4,256]{3,2,0,1:T(4,128)}, u32[]{:S(2)}, u32[]{:S(2)}) %all-to-all-start.3) | async-done | bytes 1048608 | tf_op jit(solution)/shard_map/all_to_all | solution.py:111
  273.9 8.3 %while.46 = (s32[]{:T(128)}, f32[8,128,256]{2,0,1:T(8,128)S(1)}, f32[4,128,256]{2,0,1:T(4,128)S(1)}, s32[]{:T(128)}, s32[32]{0:T(128)S(1)}, /*index=5*/s32[]{:T(...) while((s32[]{:T(128)}, f32[8,128,256]{2,0,1:T(8,128)S(1)}, ...), condition=%wide.region_7.13_spmd.clone, body=%wide.region_6.12_spmd.clone.sunk | while | flops 241716768 | bytes 12663721 | solution.py:84
  274.6 1.5 gather_fusion.4
  279.0 1.4 convolution_add_fusion.15
  280.8 1.3 convolution_add_fusion.14
  283.1 1.4 fusion.77
  284.8 84.1 %all-reduce.6.cloned.1.call-done = f32[512,256]{1,0:T(8,128)} async-done(((f32[512,256]{1,0:T(8,128)}), f32[512,256]{1,0:T(8,128)}) %all-reduce.6.cloned.1.call-update) | async-done | bytes 524304 | tf_op jit(solution)/shard_map/psum | solution.py:32
  368.9 1.2 multiply_subtract_fusion.1
  370.4 1.2 pad_maximum_fusion.2
  371.7 12.2 %all-to-all-start.4 = ((f32[2,128,4,256]{3,2,0,1:T(4,128)}), f32[2,128,4,256]{3,2,0,1:T(4,128)S(1)}, u32[]{:S(2)}, u32[]{:S(2)}) async-start(f32[2,128,4,256]{3,2,0,1:T(4,128)} %pad_maximum_fusion.2), calls=%async_computation.4 | async-start | bytes 2097152 | tf_op jit(solution)/shard_map/all_to_all | solution.py:109
  384.0 28.4 %all-to-all-done.4 = f32[2,128,4,256]{3,2,0,1:T(4,128)S(1)} async-done(((f32[2,128,4,256]{3,2,0,1:T(4,128)}), f32[2,128,4,256]{3,2,0,1:T(4,128)S(1)}, u32[]{:S(2)}, u32[]{:S(2)}) %all-to-all-start.4) | async-done | bytes 1048608 | tf_op jit(solution)/shard_map/all_to_all | solution.py:109
  413.6 1.3 select_bitcast_fusion
  414.8 8.5 %all-to-all-start.5 = ((f32[2,128,4,256]{3,2,0,1:T(4,128)}), f32[2,128,4,256]{3,2,0,1:T(4,128)}, u32[]{:S(2)}, u32[]{:S(2)}) async-start(f32[2,128,4,256]{3,2,0,1:T(4,128)} %select_bitcast_fusion), calls=%async_computation.5 | async-start | bytes 2097152 | tf_op jit(solution)/shard_map/all_to_all | solution.py:111
  425.5 1.3 fusion.74
  426.8 23.1 %all-to-all-done.5 = f32[2,128,4,256]{3,2,0,1:T(4,128)} async-done(((f32[2,128,4,256]{3,2,0,1:T(4,128)}), f32[2,128,4,256]{3,2,0,1:T(4,128)}, u32[]{:S(2)}, u32[]{:S(2)}) %all-to-all-start.5) | async-done | bytes 1048608 | tf_op jit(solution)/shard_map/all_to_all | solution.py:111
  451.3 16.5 %while.47 = (s32[]{:T(128)}, f32[8,128,256]{2,0,1:T(8,128)S(1)}, f32[4,128,256]{2,0,1:T(4,128)S(1)}, s32[]{:T(128)}, s32[32]{0:T(128)S(1)}, /*index=5*/s32[]{:T(...) while((s32[]{:T(128)}, f32[8,128,256]{2,0,1:T(8,128)S(1)}, ...), condition=%wide.region_12.18_spmd.clone, body=%wide.region_11.17_spmd.clone.sunk | while | flops 241716768 | bytes 12663721 | solution.py:84
  452.0 1.5 gather_fusion.8
  456.4 1.4 convolution_add_fusion.17
  458.2 1.3 convolution_add_fusion.16
  460.2 1.5 gather_fusion.8
  464.6 1.4 convolution_add_fusion.17
  466.4 1.3 convolution_add_fusion.16
  468.7 1.4 fusion.76
  471.9 1.3 divide_subtract_fusion
  473.2 73.2 %all-reduce.8.cloned.1.call-done = f32[512,256]{1,0:T(8,128)} async-done(((f32[512,256]{1,0:T(8,128)}), f32[512,256]{1,0:T(8,128)}) %all-reduce.8.cloned.1.call-update) | async-done | bytes 524304 | tf_op jit(solution)/shard_map/psum | solution.py:32
  546.4 2.0 multiply_subtract_fusion
  (186 shorter events, 38.9 us)
Async XLA Ops:
  7.2 1.3 copy-start.9
  9.8 17.9 %copy-start.13 = (s32[3,128]{1,0:T(4,128)S(1)}, s32[3,128]{1,0:T(4,128)}, u32[]{:S(2)}) copy-start(s32[3,128]{1,0:T(4,128)} %param.28) | copy-start | bytes 4612
  9.8 45.9 %all-to-all-start = ((f32[2,128,4,256]{3,2,0,1:T(4,128)}), f32[2,128,4,256]{3,2,0,1:T(4,128)S(1)}, u32[]{:S(2)}, u32[]{:S(2)}) async-start(f32[2,128,4,256]{3,2,0,1:T(4,128)} %pad_maximum_fusion), calls=%async_computation | async-start | bytes 2097152 | tf_op jit(solution)/shard_map/all_to_all | solution.py:109
  58.4 8.7 %copy-start.11 = (s32[3,1,1]{0,2,1:T(1,128)S(1)}, s32[3,1,1]{0,2,1:T(1,128)}, u32[]{:S(2)}) copy-start(s32[3,1,1]{0,2,1:T(1,128)} %param.30) | copy-start | bytes 40
  58.4 10.0 %copy-start = (f32[1024,256]{1,0:T(8,128)S(1)}, f32[1024,256]{1,0:T(8,128)}, u32[]{:S(2)}) copy-start(f32[1024,256]{1,0:T(8,128)} %param.24) | copy-start | bytes 3145732
  58.4 35.8 %all-to-all-start.1 = ((f32[2,128,4,256]{3,2,0,1:T(4,128)}), f32[2,128,4,256]{3,2,0,1:T(4,128)S(1)}, u32[]{:S(2)}, u32[]{:S(2)}) async-start(f32[2,128,4,256]{3,2,0,1:T(4,128)} %select_bitcast_fusion.2), calls=%async_computation.1 | async-start | bytes 2097152 | tf_op jit(solution)/shard_map/all_to_all | solution.py:111
  67.0 124.4 %all-reduce.4.cloned.1.call-start = ((), (), s32[]{:S(2)}) async-start(), calls=%async_computation.6 | async-start | bytes 1048576 | tf_op jit(solution)/shard_map/psum | solution.py:32
  68.4 1.2 copy-start.8
  68.5 0.7 copy-start.12
  94.2 1.0 copy-start.4
  95.3 0.7 copy-start.6
  101.3 1.3 copy-start.7
  102.7 0.7 copy-start.6
  108.7 1.3 copy-start.7
  110.0 1.4 copy-start.5
  194.2 40.7 %all-to-all-start.2 = ((f32[2,128,4,256]{3,2,0,1:T(4,128)}), f32[2,128,4,256]{3,2,0,1:T(4,128)S(1)}, u32[]{:S(2)}, u32[]{:S(2)}) async-start(f32[2,128,4,256]{3,2,0,1:T(4,128)} %pad_maximum_fusion.1), calls=%async_computation.2 | async-start | bytes 2097152 | tf_op jit(solution)/shard_map/all_to_all | solution.py:109
  237.5 35.1 %all-to-all-start.3 = ((f32[2,128,4,256]{3,2,0,1:T(4,128)}), f32[2,128,4,256]{3,2,0,1:T(4,128)}, u32[]{:S(2)}, u32[]{:S(2)}) async-start(f32[2,128,4,256]{3,2,0,1:T(4,128)} %select_bitcast_fusion.1), calls=%async_computation.3 | async-start | bytes 2097152 | tf_op jit(solution)/shard_map/all_to_all | solution.py:111
  245.9 123.0 %all-reduce.6.cloned.1.call-start = ((), (), s32[]{:S(2)}) async-start(), calls=%async_computation.7 | async-start | bytes 1048576 | tf_op jit(solution)/shard_map/psum | solution.py:32
  246.7 1.2 copy-start.1
  247.9 0.7 copy-start.10
  371.7 40.7 %all-to-all-start.4 = ((f32[2,128,4,256]{3,2,0,1:T(4,128)}), f32[2,128,4,256]{3,2,0,1:T(4,128)S(1)}, u32[]{:S(2)}, u32[]{:S(2)}) async-start(f32[2,128,4,256]{3,2,0,1:T(4,128)} %pad_maximum_fusion.2), calls=%async_computation.4 | async-start | bytes 2097152 | tf_op jit(solution)/shard_map/all_to_all | solution.py:109
  414.8 35.1 %all-to-all-start.5 = ((f32[2,128,4,256]{3,2,0,1:T(4,128)}), f32[2,128,4,256]{3,2,0,1:T(4,128)}, u32[]{:S(2)}, u32[]{:S(2)}) async-start(f32[2,128,4,256]{3,2,0,1:T(4,128)} %select_bitcast_fusion), calls=%async_computation.5 | async-start | bytes 2097152 | tf_op jit(solution)/shard_map/all_to_all | solution.py:111
  423.3 123.1 %all-reduce.8.cloned.1.call-start = ((), (), s32[]{:S(2)}) async-start(), calls=%async_computation.8 | async-start | bytes 1048576 | tf_op jit(solution)/shard_map/psum | solution.py:32
  424.0 1.2 copy-start.3
  470.4 1.2 copy-start.2
Sparse Core Ops, SparseCore 0:
  111.1 80.3 all-reduce.3
  283.2 85.7 all-reduce.5
  468.8 77.5 all-reduce.7
where the time goes:
time: 556 us; the launch traced here: 555 us
  waiting for transfers between devices  391 us (70%)
  starting transfers between devices  67.8 us (12%)
  local copies, waits for them, and re-layouts  38.7 us (7%)
  other arithmetic  21 us (4%)
  matrix products  19.4 us (3%)
  between operations  16.4 us (3%)
    psum x3, waiting for transfers between devices, rep_total(): return lax.psum(item_part, 'rep')  237 us
    all_to_all x3, waiting for transfers between devices, on_device(): lax.all_to_all(pieces, 'stratum', split_axis=1, concat_axis=1, tiled=True)  84.6 us
    all_to_all x3, waiting for transfers between devices, on_device(): lax.all_to_all(ordered, 'stratum', split_axis=1, concat_axis=1, tiled=True)  69.4 us
    all_to_all x3, starting transfers between devices, on_device(): lax.all_to_all(pieces, 'stratum', split_axis=1, concat_axis=1, tiled=True)  42.2 us
    all_to_all x3, starting transfers between devices, on_device(): lax.all_to_all(ordered, 'stratum', split_axis=1, concat_axis=1, tiled=True)  25.5 us
  transfers between devices with their start and end apart: 9, of which 9 were waited for; matrix products, arithmetic and copies ran while one was open for 2% of the time, Pallas kernels for 0%

commit v1 on v0

v1 whole, which is shorter than its diff:
```python
import jax
import jax.numpy as jnp
from jax import lax
from jax.experimental import pallas as pl
from jax.experimental.pallas import tpu as pltpu
from jax.sharding import PartitionSpec as P

STRATA = 3
SHRINKAGE = 0.02
RATE_START = 0.25
RATE_DECAY = 0.75

NX, NY, NZ = 4, 8, 4
POS = NX * NY * NZ
SEMS = 176

F32 = jnp.float32
BF16 = jnp.bfloat16
MESH = pl.DeviceIdType.MESH
NT = (((1,), (1,)), ((), ()))
TN = (((0,), (0,)), ((), ()))


def dot(a, b):
    return jnp.dot(a, b, preferred_element_type=F32)


def iota(shape, axis):
    return lax.broadcasted_iota(jnp.int32, shape, axis)


def order_a(o):
    return ((o // 4) % 4) * 32 + (o // 16) * 4 + o % 4


def order_b(o):
    return ((o // 4) % 8) * 16 + (o % 4) * 4 + o // 32


def kernel(
    user_hbm, uacc_ref, item_hbm, iacc_hbm, move_ref, list_ref, count_ref, bits_hbm,
    user_out, item_out,
    xs, xl, ucol, words, cat, wsort, usort, mask, err, part, yl, yh, ah, onehot, perm, rows_in, acc_in, items_new,
    sp_s, sp_zr, sp_yr, sp_xr,
    ac_s, ac_zr, ac_yr, ac_xr,
    ou_s, ou_xr, ou_yr, ou_cr,
    fa_s, fa_xr, fa_yr, fa_zr,
    bk_cr, bk_z, bk_zr, bk_s, bk_yr, bk_xr,
    fin_s, fin_r, fin_new,
    local_sem, send_sem, recv_sem,
):
    s = lax.axis_index("stratum")
    r = lax.axis_index("rep")
    x = lax.rem(s, 4)
    zl = lax.rem(s // 4, 4)
    y = s // 16
    c = lax.rem(r, 2)
    zh = r // 2
    z = zh * 4 + zl

    def dev_x(v):
        return (y * 16 + zl * 4 + v, r)

    def dev_y(v):
        return (v * 16 + zl * 4 + x, r)

    def dev_zl(v):
        return (y * 16 + v * 4 + x, r)

    def dev_z(v):
        return (y * 16 + lax.rem(v, 4) * 4 + x, (v // 4) * 2 + c)

    other_core = (s, zh * 2 + (1 - c))
    other_zh = (s, (1 - zh) * 2 + c)

    used = [0]
    pending = []

    def send(src, dst, device):
        k = used[0]
        used[0] = k + 1
        copy = pltpu.make_async_remote_copy(
            src_ref=src, dst_ref=dst, send_sem=send_sem.at[k], recv_sem=recv_sem.at[k],
            device_id=device, device_id_type=MESH,
        )
        copy.start()
        pending.append(copy)
        return copy

    far_first = {4: (2, 1, 3), 8: (4, 3, 5, 2, 6, 1, 7)}

    def exchange(n, me, device_of, src_at, recv):
        copies = {}
        for k in far_first[n]:
            peer = lax.rem(me + k, n)
            copies[k] = send(src_at(peer), recv.at[me], device_of(peer))
        recv[me] = src_at(me)[...]
        return copies

    def arrive(copies):
        for k in sorted(copies, key=lambda k: min(k, len(copies) + 1 - k)):
            copies[k].wait_recv()

    def drain():
        for copy in pending:
            copy.wait_send()
        pending.clear()

    quarter = pl.multiple_of(c * 256 + zh * 128, 128)
    loads = [
        pltpu.make_async_copy(item_hbm.at[pl.ds(quarter, 128)], rows_in, local_sem.at[0]),
        pltpu.make_async_copy(iacc_hbm.at[pl.ds(quarter, 128)], acc_in, local_sem.at[1]),
        pltpu.make_async_copy(user_hbm, xs, local_sem.at[2]),
    ] + [
        pltpu.make_async_copy(bits_hbm.at[t, 0, 0], words.at[t], local_sem.at[3 + t]) for t in range(STRATA)
    ]
    for load in loads:
        load.start()

    barrier = pltpu.get_barrier_semaphore()
    peers = (
        [dev_x(lax.rem(x + k, 4)) for k in range(1, 4)]
        + [dev_y(lax.rem(y + k, 8)) for k in range(1, 8)]
        + [dev_z(lax.rem(z + k, 8)) for k in range(1, 8)]
        + [other_core]
    )
    for peer in peers:
        pl.semaphore_signal(barrier, inc=1, device_id=peer, device_id_type=MESH)

    row = iota((POS, POS), 0)
    col = iota((POS, POS), 1)
    perm[0] = (order_a(row) == col).astype(BF16)
    perm[1] = (order_b(row) == col).astype(BF16)

    def reorder(which, array):
        return dot(perm[which], array).astype(BF16)

    loads[0].wait()
    sp_s[0] = rows_in[...].astype(BF16).reshape(4, 32, 256)
    pl.semaphore_wait(barrier, len(peers))

    rows_z = exchange(4, zl, dev_zl, lambda v: sp_s.at[0, v], sp_zr)
    loads[1].wait()
    ac_s[0] = acc_in[...].astype(BF16).reshape(4, 32, 256)
    accs_z = exchange(4, zl, dev_zl, lambda v: ac_s.at[0, v], ac_zr)

    chain = (order_b(col) == row).astype(BF16)
    for t in range(STRATA):
        move = move_ref[pl.ds(t, 1), :]
        onehot[t] = dot((move == order_b(row)).astype(BF16), chain).astype(BF16)
        if t + 1 < STRATA:
            chain = dot((move == row).astype(BF16), chain).astype(BF16)

    arrive(rows_z)
    sp_s[1] = reorder(0, sp_zr[...].reshape(POS, 256)).reshape(4, 32, 256)
    rows_y = exchange(8, y, dev_y, lambda v: sp_s.at[1, v // 2, pl.ds(pl.multiple_of(lax.rem(v, 2) * 16, 16), 16)], sp_yr)
    arrive(accs_z)
    ac_s[1] = reorder(0, ac_zr[...].reshape(POS, 256)).reshape(4, 32, 256)
    accs_y = exchange(8, y, dev_y, lambda v: ac_s.at[1, v // 2, pl.ds(pl.multiple_of(lax.rem(v, 2) * 16, 16), 16)], ac_yr)

    loads[2].wait()
    xl[...] = xs[...].astype(BF16)
    for a in range(8):
        line = jnp.broadcast_to(uacc_ref[pl.ds(a, 1), :], (128, 128))
        ucol[pl.ds(a * 128, 128), :] = jnp.sum(jnp.where(row == col, line, 0.0), axis=1, keepdims=True)

    def sort_words(t):
        loads[3 + t].wait()
        cat[:, 0:128] = words[t].reshape(512, 128).astype(F32).astype(BF16)
        cat[:, 128:256] = jnp.ones((512, 128), BF16)
        spread = (iota((32, 512), 1) // 16 == iota((32, 512), 0)).astype(BF16)
        slots = jnp.broadcast_to(list_ref[t, 0].astype(F32).astype(BF16), (8, 32))
        slot_of = dot(slots, spread)[0:1, :].astype(jnp.int32)
        lane = iota((1, 512), 1)
        slot_of = jnp.where(lane // 16 < count_ref[t, 0, 0], slot_of * 16 + lane % 16, -1)
        for a in range(4):
            pick = (slot_of == iota((128, 512), 0) + a * 128).astype(BF16)
            got = dot(pick, cat[...])
            wsort[pl.ds(a * 128, 128), :] = got[:, 0:128].astype(jnp.int32)
            usort[pl.ds(a * 128, 128), :] = got[:, 128:256]

    def fill_mask():
        shift = iota((8, 128), 0)

        def one_slot(slot, carry):
            base = slot * 16
            at_row = pl.multiple_of(lax.rem(slot, 4) * 128, 128)
            at_col = pl.multiple_of((slot // 4) * 128, 128)
            on = jnp.broadcast_to(usort[pl.ds(base, 1), :], (8, 128))
            for w in range(0, 16, 2):
                both = []
                for v in (w, w + 1):
                    line = jnp.broadcast_to(wsort[pl.ds(base + v, 1), :], (8, 128))
                    bit = jnp.bitwise_and(jnp.right_shift(line, shift), 1).astype(F32)
                    both.append(on + 2.0 * bit)
                mask[pl.ds(at_row + w * 8, 16), pl.ds(at_col, 128)] = jnp.concatenate(both, axis=0).astype(BF16)
            return carry

        lax.fori_loop(0, 32, one_slot, 0)

    arrive(rows_y)
    sp_s[2] = reorder(1, sp_yr[...].reshape(POS, 256)).reshape(4, 32, 256)
    rows_x = exchange(4, x, dev_x, lambda v: sp_s.at[2, v], sp_xr)
    arrive(accs_y)
    ac_s[2] = reorder(1, ac_yr[...].reshape(POS, 256)).reshape(4, 32, 256)
    accs_x = exchange(4, x, dev_x, lambda v: ac_s.at[2, v], ac_xr)
    sort_words(0)
    arrive(rows_x)
    home = sp_xr[...].reshape(POS, 256)
    yh[...] = home.astype(F32)

    for t in range(STRATA):
        last = t == STRATA - 1
        rate = RATE_START * RATE_DECAY**t
        ou_s[t, 0] = dot(onehot[t], yh[...].astype(BF16)).astype(BF16).reshape(4, 32, 256)
        out_x = exchange(4, x, dev_x, lambda v: ou_s.at[t, 0, v], ou_xr.at[t])
        if last:
            fa_s[0] = dot(onehot[t], ah[...].astype(BF16)).astype(BF16).reshape(4, 32, 256)
            fa_x = exchange(4, x, dev_x, lambda v: fa_s.at[0, v], fa_xr)
        if t == 0:
            arrive(accs_x)
            ah[...] = ac_xr[...].reshape(POS, 256).astype(F32)
            fill_mask()
        drain()
        arrive(out_x)
        ou_s[t, 1] = reorder(0, ou_xr[t].reshape(POS, 256)).reshape(4, 32, 256)
        out_y = exchange(
            8, y, dev_y, lambda v: ou_s.at[t, 1, v // 2, pl.ds(pl.multiple_of(lax.rem(v, 2) * 16, 16), 16)], ou_yr.at[t]
        )
        if last:
            arrive(fa_x)
            fa_s[1] = reorder(0, fa_xr[...].reshape(POS, 256)).reshape(4, 32, 256)
        arrive(out_y)
        ou_s[t, 2] = reorder(1, ou_yr[t].reshape(POS, 256)).reshape(4, 32, 256)
        half = yl.at[t, c]
        out_z = exchange(8, z, dev_z, lambda v: ou_s.at[t, 2, lax.rem(v, 4)], half)
        if last:
            fa_y = exchange(
                8, y, dev_y, lambda v: fa_s.at[1, v // 2, pl.ds(pl.multiple_of(lax.rem(v, 2) * 16, 16), 16)], fa_yr
            )
        over = [send(half.at[z], yl.at[t, c, z], other_core)]
        for k in (1, 7, 2, 6, 3, 5, 4):
            out_z[k].wait_recv()
            piece = lax.rem(z + 8 - k, 8)
            over.append(send(half.at[piece], yl.at[t, c, piece], other_core))
        if last:
            arrive(fa_y)
            fa_s[2] = reorder(1, fa_yr[...].reshape(POS, 256)).reshape(4, 32, 256)
            fa_z = exchange(4, zl, dev_zl, lambda v: fa_s.at[2, v], fa_zr)
        for copy in over:
            copy.wait_recv()

        def item_chunk(h, q):
            items = yl[t, h, pl.ds(q * 4, 4)].reshape(128, 256)
            at = pl.multiple_of(h * 256 + q * 128, 128)
            scores = lax.dot_general(items, xl[...], NT, preferred_element_type=F32)
            weight = mask[pl.ds(at, 128), :].astype(F32)
            e = (weight * (scores - jnp.where(weight > 2.0, 1.0, 0.0))).astype(BF16)
            err[pl.ds(at, 128), :] = e
            return dot(e, xl[...])

        for q in range(2):
            part[0, pl.ds(q * 128, 128), :] = item_chunk(1 - c, q)
        swap = send(part.at[0], bk_cr.at[t], other_core)
        for q in range(2):
            part[1, pl.ds(q * 128, 128), :] = item_chunk(c, q)
        swap.wait_recv()
        both = part[1] + bk_cr[t]

        def users():
            items = yl[t].reshape(512, 256)
            for u in range(4):
                at = pl.ds(u * 256, 256)
                old = xs[at, :]
                grad = lax.dot_general(err[:, u * 256 : u * 256 + 256], items, TN, preferred_element_type=F32)
                grad = grad + SHRINKAGE * old
                acc = ucol[at, :] + jnp.sum(grad * grad, axis=1, keepdims=True) * (1.0 / 256.0)
                ucol[at, :] = acc
                new = old - grad * (rate / jnp.sqrt(acc))
                xs[at, :] = new
                if not last:
                    xl[at, :] = new.astype(BF16)

        if not last:
            bk_z[t] = both.astype(BF16).reshape(8, 32, 256)
            back_z = exchange(8, z, dev_z, lambda v: bk_z.at[t, v], bk_zr.at[t])
            users()
            drain()
            arrive(back_z)
            near = bk_zr[t, 0:4].reshape(POS, 256)
            away = bk_zr[t, 4:8].reshape(POS, 256)
            bk_s[t, 0] = (dot(perm[0], near) + dot(perm[0], away)).astype(BF16).reshape(4, 32, 256)
            back_y = exchange(
                8, y, dev_y, lambda v: bk_s.at[t, 0, v // 2, pl.ds(pl.multiple_of(lax.rem(v, 2) * 16, 16), 16)], bk_yr.at[t]
            )
            sort_words(t + 1)
            arrive(back_y)
            bk_s[t, 1] = reorder(1, bk_yr[t].reshape(POS, 256)).reshape(4, 32, 256)
            back_x = exchange(4, x, dev_x, lambda v: bk_s.at[t, 1, v], bk_xr.at[t])
            fill_mask()
            arrive(back_x)
            grad = lax.dot_general(onehot[t], bk_xr[t].reshape(POS, 256), TN, preferred_element_type=F32)
            grad = grad + SHRINKAGE * yh[...]
            acc = ah[...] + grad * grad
            ah[...] = acc
            yh[...] = yh[...] - rate * grad / jnp.sqrt(acc)
        else:
            part[1] = both
            fin_s[...] = part[1, pl.ds(pl.multiple_of((1 - zh) * 128, 128), 128), :].astype(BF16)
            cross = send(fin_s, fin_r, other_zh)
            users()
            store = pltpu.make_async_copy(xs, user_out, local_sem.at[6])
            store.start()
            arrive(fa_z)
            old = yl[t, c, pl.ds(zh * 4, 4)].reshape(128, 256).astype(F32)
            before = fa_zr[...].reshape(128, 256).astype(F32)
            cross.wait_recv()
            grad = part[1, pl.ds(pl.multiple_of(zh * 128, 128), 128), :] + fin_r[...].astype(F32)
            grad = grad + SHRINKAGE * old
            new = old - rate * grad / jnp.sqrt(before + grad * grad)
            fin_new[c, zh] = new.astype(BF16)
            mine = fin_new.at[c, zh]
            gather = [send(mine, fin_new.at[c, zh], other_zh), send(mine, fin_new.at[c, zh], other_core)]
            gather[0].wait_recv()
            theirs = fin_new.at[c, 1 - zh]
            gather.append(send(theirs, fin_new.at[c, 1 - zh], other_core))
            drain()
            gather[1].wait_recv()
            gather[2].wait_recv()
            items_new[...] = fin_new[...].reshape(512, 256).astype(F32)
            done = pltpu.make_async_copy(items_new, item_out, local_sem.at[7])
            done.start()
            store.wait()
            done.wait()


def on_device(
    user_rows, user_accum, item_rows, item_accum, move_lists, tile_lists, tile_counts, rating_bits
):
    vmem, smem, anywhere = (
        pl.BlockSpec(memory_space=pltpu.VMEM), pl.BlockSpec(memory_space=pltpu.SMEM), pl.BlockSpec(memory_space=pl.ANY),
    )
    v = pltpu.VMEM
    stage, wide = (4, 32, 256), (8, 16, 256)
    new_users, new_items = pl.pallas_call(
        kernel,
        out_shape=(
            jax.ShapeDtypeStruct((1024, 256), F32),
            jax.ShapeDtypeStruct((512, 256), F32),
        ),
        in_specs=[anywhere, vmem, anywhere, anywhere, vmem, vmem, smem, anywhere],
        out_specs=(anywhere, anywhere),
        scratch_shapes=[
            v((1024, 256), F32), v((1024, 256), BF16), v((1024, 1), F32),
            v((STRATA, 32, 16, 128), jnp.int32), v((512, 256), BF16), v((512, 128), jnp.int32), v((512, 128), F32),
            v((512, 1024), BF16), v((512, 1024), BF16), v((2, 256, 256), F32), v((STRATA, 2, 8, 32, 256), BF16),
            v((POS, 256), F32), v((POS, 256), F32), v((STRATA, POS, POS), BF16), v((2, POS, POS), BF16),
            v((128, 256), F32), v((128, 256), F32), v((512, 256), F32),
            v((3, *stage), BF16), v(stage, BF16), v(wide, BF16), v(stage, BF16),
            v((3, *stage), BF16), v(stage, BF16), v(wide, BF16), v(stage, BF16),
            v((STRATA, 3, *stage), BF16), v((STRATA, *stage), BF16), v((STRATA, *wide), BF16), v((8, 128), F32),
            v((3, *stage), BF16), v(stage, BF16), v(wide, BF16), v(stage, BF16),
            v((STRATA, 256, 256), F32), v((2, 8, 32, 256), BF16), v((2, 8, 32, 256), BF16),
            v((2, 2, *stage), BF16), v((2, *wide), BF16), v((2, *stage), BF16),
            v((128, 256), BF16), v((128, 256), BF16), v((2, 2, 128, 256), BF16),
            pltpu.SemaphoreType.DMA((8,)),
            pltpu.SemaphoreType.DMA((SEMS,)),
            pltpu.SemaphoreType.DMA((SEMS,)),
        ],
        compiler_params=pltpu.CompilerParams(
            collective_id=0, has_side_effects=True, vmem_limit_bytes=48 * 1024 * 1024
        ),
        cost_estimate=pl.CostEstimate(flops=3 * 3 * 2 * 1024 * 512 * 256, bytes_accessed=6 * 1024 * 1024, transcendentals=0),
    )(user_rows, user_accum.reshape(8, 128), item_rows, item_accum, move_lists, tile_lists, tile_counts, rating_bits)
    return new_users, new_items


def solution(mesh):
    in_specs = (
        P(("stratum", "rep"), None),
        P(("stratum", "rep")),
        P("stratum", None),
        P("stratum", None),
        P(),
        P(None, "stratum", "rep", None),
        P(None, "stratum", "rep"),
        P(None, "stratum", "rep", None, None, None),
    )
    out_specs = (P(("stratum", "rep"), None), P("stratum", None))
    return jax.shard_map(
        on_device, mesh=mesh, in_specs=in_specs, out_specs=out_specs, check_vma=False
    )
```

time: 556 us -> 132 us (0.24)
  waiting for transfers between devices: 391 us -> 0 us
  Pallas kernels: 0 us -> 123 us
  starting transfers between devices: 67.8 us -> 0 us
  local copies, waits for them, and re-layouts: 38.7 us -> 7.65 us
  other arithmetic: 21 us -> 0 us
  matrix products: 19.4 us -> 0 us
  between operations: 16.4 us -> 0.66 us
    psum x3 -> x0, waiting for transfers between devices: 237 us -> none  [rep_total(): return lax.psum(item_part, 'rep')]
    all_to_all x6 -> x0, waiting for transfers between devices: 154 us -> none  [the longest x3 84.6 us: on_device(): lax.all_to_all(pieces, 'stratum', split_axis=1, concat_axis=1, tiled=True)]
    pallas_call x0 -> x1, Pallas kernels: none -> 123 us  [on_device(): pl.pallas_call(kernel, out_shape=(jax.ShapeDtypeStruct((1024, 256), F32),...]
    all_to_all x6 -> x0, starting transfers between devices: 67.7 us -> none  [the longest x3 42.2 us: on_device(): lax.all_to_all(pieces, 'stratum', split_axis=1, concat_axis=1, tiled=True)]
    dot_general x25 -> x0, matrix products: 19.4 us -> none  [the longest x5 7.12 us: one_group(): jnp.einsum('gc,gir->cir', col_hot, item_part, precision=lax.Precision.HIG...]
    gather x23 -> x0, local copies, waits for them, and re-layouts: 18.2 us -> none  [the longest x5 5.61 us: one_group(): observed = unpack_bits(jnp.take(bit_words, clamped, axis=0))]
    convert_element_type x8 -> x0, other arithmetic: 6.07 us -> none  [the longest x5 3.43 us: one_group(): active = (position < tile_count).astype(jnp.float32)]
    slice x7 -> x0, local copies, waits for them, and re-layouts: 5.97 us -> none  [the longest x5 3.92 us: on_device(): item_low = item_state[0].astype(jnp.bfloat16)]
  transfers between devices with their start and end apart: 9 -> 0, of which waited for: 9 -> 0; matrix products, arithmetic and copies ran while one was open for 2% -> 0% of each run, Pallas kernels for 0% -> 0%
where the time goes in v1:
time: 132 us
  Pallas kernels  123 us (93%)
  local copies, waits for them, and re-layouts  7.65 us (6%)
    pallas_call x1, Pallas kernels, on_device(): pl.pallas_call(kernel, out_shape=(jax.ShapeDtypeStruct((1024, 256), F32),...  123 us
    unnamed x17, local copies, waits for them, and re-layouts  7.65 us

profile of v1, /device:TPU:1, one launch (start us, length us, event | category | flops | bytes accessed | tf_op | source)
XLA Modules:
  0.0 131.7 jit_solution(2131937083651920231)
XLA Ops:
  0.6 0.0 copy-start.6
  0.6 0.0 copy-start.5
  0.7 0.8 copy.10.count_ref
  1.4 0.0 copy-done.6
  1.4 0.0 copy-done.5
  1.4 0.0 copy-start
  1.4 1.2 copy-done
  2.6 0.0 copy-start.1
  2.6 1.1 copy-done.1
  3.8 0.0 copy-start.2
  3.8 1.0 copy-done.2
  4.8 0.0 copy-start.3
  4.8 1.0 copy-done.3
  5.9 0.0 copy-start.4
  5.9 0.7 copy-done.4
  6.5 123.4 %shard_map.95 = (f32[1024,256]{1,0:T(8,128)S(1)}, f32[512,256]{1,0:T(8,128)S(1)}) custom-call(f32[1024,256]{1,0:T(8,128)S(1)} %copy-done, f32[8,128]{1,0:T(8,128)S(1)} %bitcast.1, f32[512,256]{1,0:T(8,128)S(1)} %copy-done.2, f32[512,256]{1,0:T(8,128)S(1)} %copy-done.3, s32[3,128]{1,0:T(4,128)S(1)} %copy-done.5, s32[3,1,1,32]{3,2,1,0:T(1,128)S(1)} %copy-done.6, ...), custom_call_target="tpu_custom_call" | custom-call | flops 2415919104 | bytes 6291456 | tf_op jit(solution)/shard_map/pallas_call | solution.py:345
  129.9 1.0 copy.13
  130.9 0.8 copy.14
Async XLA Ops:
  0.6 0.8 copy-start.6
  0.6 0.8 copy-start.5
  1.4 1.2 copy-start
  2.6 1.1 copy-start.1
  3.8 1.0 copy-start.2
  4.8 1.0 copy-start.3
  5.9 0.7 copy-start.4

commit v2 on v0

v2 whole, which is shorter than its diff:
```python
import jax
import jax.numpy as jnp
from jax import lax
from jax.experimental import pallas as pl
from jax.experimental.pallas import tpu as pltpu
from jax.sharding import PartitionSpec as P

STRATA = 3
SHRINKAGE = 0.02
RATE_START = 0.25
RATE_DECAY = 0.75

F32 = jnp.float32
BF16 = jnp.bfloat16
MESH = pl.DeviceIdType.MESH
NT = (((1,), (1,)), ((), ()))
TN = (((0,), (0,)), ((), ()))
X_ORDER = (0, 1, 3, 2)


def dot(a, b):
    return jnp.dot(a, b, preferred_element_type=F32)


def iota(shape, axis):
    return lax.broadcasted_iota(jnp.int32, shape, axis)


def natural(d):
    return (d // 16) * 16 + (d % 4) * 4 + (d // 4) % 4


def rows_at(index, size):
    return pl.ds(pl.multiple_of(index * size, size), size)


def kernel(
    user_hbm, uacc_hbm, item_hbm, iacc_hbm, move_hbm, list_hbm, count_ref, bits_hbm,
    user_out, item_out,
    xs, xl, uacc_ref, ucol, move_ref, list_ref, words, cat, wsort, usort, mask, err, yl, part, yh, ah,
    onehot, onehot_t, perm, perm_sum, rows_in, acc_in, items_new,
    sp_n, sp_s, sp_yr, sp_zr,
    ac_n, ac_s, ac_yr, ac_zr,
    ou_s, ou_yr,
    fa_s, fa_yr, fa_zr,
    bk_cr, bk_z, bk_zr, bk_s, bk_yr,
    fin_s, fin_r,
    local_sem, send_sem, recv_sem, line_sem,
):
    s = lax.axis_index("stratum")
    r = lax.axis_index("rep")
    x = lax.rem(s, 4)
    zl = lax.rem(s // 4, 4)
    y = s // 16
    c = lax.rem(r, 2)
    zh = r // 2
    z = zh * 4 + zl
    half = pl.ds(pl.multiple_of(c * 128, 128), 128)
    other_half = pl.ds(pl.multiple_of((1 - c) * 128, 128), 128)

    def dev(xv, yv, zv):
        return (yv * 16 + lax.rem(zv, 4) * 4 + xv, (zv // 4) * 2 + c)

    other_core = (s, zh * 2 + (1 - c))
    other_zh = (s, (1 - zh) * 2 + c)

    loads = []

    def load(src, dst):
        copy = pltpu.make_async_copy(src, dst, local_sem.at[len(loads)])
        loads.append(copy)
        copy.start()
        return copy

    load_rows = load(item_hbm.at[:, half], rows_in)
    load_acc = load(iacc_hbm.at[:, half], acc_in)
    load_move = load(move_hbm, move_ref)
    load_list = load(list_hbm, list_ref)
    load_bits = [load(bits_hbm.at[0, 0, 0], words.at[0])]
    load_uacc = load(uacc_hbm, uacc_ref)
    load_user = load(user_hbm, xs)
    load_bits += [load(bits_hbm.at[t, 0, 0], words.at[t]) for t in (1, 2)]

    barrier = pltpu.get_barrier_semaphore()
    x_peers = [dev(lax.rem(x + k, 4), y, z) for k in (2, 1, 3)]
    y_peers = [dev(x, lax.rem(y + k, 8), z) for k in (4, 3, 5, 2, 6, 1, 7)]
    z_peers = [dev(x, y, lax.rem(z + k, 8)) for k in (4, 3, 5, 2, 6, 1, 7)]
    peers = y_peers + z_peers + x_peers + [other_core]
    for peer in peers:
        pl.semaphore_signal(barrier, inc=1, device_id=peer, device_id_type=MESH)

    sends = []
    arrivals = [0]

    def take(ref):
        k = len(sends)
        sends.append(ref)
        return send_sem.at[k]

    def arrival():
        k = arrivals[0]
        arrivals[0] = k + 1
        return recv_sem.at[k]

    def send(src, dst, sent, landed, device):
        pltpu.make_async_remote_copy(
            src_ref=src, dst_ref=dst, send_sem=sent, recv_sem=landed, device_id=device, device_id_type=MESH
        ).start()

    def wait(ref, sem):
        pltpu.make_async_copy(ref, ref, sem).wait()

    def along_y(src, recv):
        sent, landed = take(recv.at[pl.ds(0, 7)]), arrival()
        for k in (4, 3, 5, 2, 6, 1, 7):
            peer = lax.rem(y + k, 8)
            send(src.at[peer], recv.at[y], sent, landed, dev(x, peer, z))
        recv[y] = src[y]
        return lambda: wait(recv.at[pl.ds(0, 7)], landed)

    def to_homes(src, recv):
        sent, landed = take(recv.at[pl.ds(0, 15)]), arrival()
        here = x * 4 + zl
        for kx in (2, 1, 3, 0):
            for k in (3, 0, 2, 1):
                if kx == 0 and k == 1:
                    continue
                px = lax.rem(x + kx, 4)
                send(src.at[px * 4 + k], recv.at[here], sent, landed, dev(px, y, lax.rem(z + 7 + k, 8)))
        recv[here] = src[x * 4 + 1]
        return lambda: wait(recv.at[pl.ds(0, 15)], landed)

    far_z = (4, 3, 5, 2, 6, 1, 7)

    def to_positions(src, recv, whole):
        sent = take(recv.at[pl.ds(0, 31 * 16), pl.ds(0, 128)] if whole else recv.at[pl.ds(0, 31)])
        here = (rows_at(x * 8 + z, 16), half) if whole else (x * 8 + z,)
        landed = {kx: arrival() for kx in X_ORDER} if whole else dict.fromkeys(X_ORDER, arrival())
        for kx in (2, 1, 3, 0):
            px = lax.rem(x + kx, 4)
            for kz in far_z + (0,):
                if kx == 0 and kz == 0:
                    continue
                pz = lax.rem(z + kz, 8)
                send(src.at[px * 4 + lax.rem(pz, 4)], recv.at[here], sent, landed[kx], dev(px, y, pz))
        recv[here] = src[x * 4 + zl]
        return landed

    row = iota((256, 256), 0)
    col = iota((256, 256), 1)
    perm[0] = ((row // 2 % 8) * 32 + (row // 16) * 2 + row % 2 == col).astype(BF16)
    perm[1] = ((col // 2 % 8) * 32 + (col // 16) * 2 + col % 2 == row).astype(BF16)

    load_rows.wait()
    for xh in range(4):
        for k in range(4):
            at = rows_at(xh * 8 + lax.rem(z + 7 + k, 8), 16)
            sp_n[pl.ds((xh * 4 + k) * 16, 16), :] = rows_in[at, :].astype(BF16)
    sp_s[0] = dot(perm[1], sp_n[...]).astype(BF16).reshape(8, 32, 128)
    pl.semaphore_wait(barrier, len(peers))

    rows_y = along_y(sp_s.at[0], sp_yr)
    for peer in x_peers:
        pl.semaphore_signal(line_sem, inc=1, device_id=peer, device_id_type=MESH)
    load_acc.wait()
    for xh in range(4):
        for k in range(4):
            at = rows_at(xh * 8 + lax.rem(z + 7 + k, 8), 16)
            ac_n[pl.ds((xh * 4 + k) * 16, 16), :] = acc_in[at, :].astype(BF16)
    ac_s[0] = dot(perm[1], ac_n[...]).astype(BF16).reshape(8, 32, 128)
    accs_y = along_y(ac_s.at[0], ac_yr)

    wide = iota((256, 512), 1)
    tall = iota((256, 512), 0)
    xz = tall // 2 % 16
    from_row = (wide // 128 == xz // 4) & (wide // 16 % 4 == xz % 4) & (wide % 16 == (tall // 32) * 2 + tall % 2)
    perm_sum[...] = from_row.astype(BF16)

    load_move.wait()
    chain = (natural(iota((128, 256), 1) // 2) == iota((128, 256), 0)).astype(BF16)
    for t in range(STRATA):
        move = move_ref[pl.ds(t, 1), :]
        to = (move == natural(iota((256, 128), 0) // 2)).astype(BF16)
        stands = jnp.where(row % 2 == col % 2, dot(to, chain), 0.0)
        onehot[t] = stands.astype(BF16)
        if t + 1 < STRATA:
            onehot_t[t] = jnp.transpose(stands).astype(BF16)
            chain = dot((move == iota((128, 128), 0)).astype(BF16), chain).astype(BF16)

    def sort_words(t):
        load_bits[t].wait()
        cat[:, 0:128] = words[t].reshape(512, 128).astype(F32).astype(BF16)
        spread = (iota((32, 512), 1) // 16 == iota((32, 512), 0)).astype(BF16)
        slots = jnp.broadcast_to(list_ref[t, 0].astype(F32).astype(BF16), (8, 32))
        slot_of = dot(slots, spread)[0:1, :].astype(jnp.int32)
        lane = iota((1, 512), 1)
        slot_of = jnp.where(lane // 16 < count_ref[0, t], slot_of * 16 + lane % 16, -1)
        for a in range(4):
            pick = (slot_of == iota((128, 512), 0) + a * 128).astype(BF16)
            got = dot(pick, cat[...])
            wsort[pl.ds(a * 128, 128), :] = got[:, 0:128].astype(jnp.int32)
            usort[pl.ds(a * 128, 128), :] = got[:, 128:256]

    def fill_mask():
        shift = iota((8, 128), 0)

        def one_slot(slot, carry):
            base = slot * 16
            at_row = pl.multiple_of(lax.rem(slot, 4) * 128, 128)
            at_col = pl.multiple_of((slot // 4) * 128, 128)
            on = jnp.broadcast_to(usort[pl.ds(base, 1), :], (8, 128))
            for w in range(0, 16, 2):
                both = []
                for v in (w, w + 1):
                    line = jnp.broadcast_to(wsort[pl.ds(base + v, 1), :], (8, 128))
                    bit = jnp.bitwise_and(jnp.right_shift(line, shift), 1).astype(F32)
                    both.append(on + 2.0 * bit)
                mask[pl.ds(at_row + w * 8, 16), pl.ds(at_col, 128)] = jnp.concatenate(both, axis=0).astype(BF16)
            return carry

        lax.fori_loop(0, 32, one_slot, 0)

    rows_y()
    pl.semaphore_wait(line_sem, len(x_peers))
    sp_s[1] = dot(perm[0], sp_yr[...].reshape(256, 128)).astype(BF16).reshape(8, 32, 128)
    rows_z = to_homes(sp_s.at[1].reshape(16, 16, 128), sp_zr)
    accs_y()
    ac_s[1] = dot(perm[0], ac_yr[...].reshape(256, 128)).astype(BF16).reshape(8, 32, 128)
    accs_z = to_homes(ac_s.at[1].reshape(16, 16, 128), ac_zr)

    cat[:, 128:256] = jnp.ones((512, 128), BF16)
    load_list.wait()
    sort_words(0)
    load_user.wait()
    xl[...] = xs[...].astype(BF16)
    load_uacc.wait()
    eye = iota((128, 128), 0) == iota((128, 128), 1)
    for a in range(8):
        line = jnp.broadcast_to(uacc_ref[pl.ds(a, 1), :], (128, 128))
        ucol[pl.ds(a * 128, 128), :] = jnp.sum(jnp.where(eye, line, 0.0), axis=1, keepdims=True)

    rows_z()
    yh[...] = dot(perm[1], sp_zr[...].reshape(256, 128))

    for t in range(STRATA):
        last = t == STRATA - 1
        rate = RATE_START * RATE_DECAY**t
        ou_s[t, 0] = dot(onehot[t], yh[...].astype(BF16)).astype(BF16).reshape(8, 32, 128)
        out_y = along_y(ou_s.at[t, 0], ou_yr.at[t])
        if last:
            fa_s[0] = dot(onehot[t], ah[...].astype(BF16)).astype(BF16).reshape(8, 32, 128)
            fa_y = along_y(fa_s.at[0], fa_yr)
        if t == 0:
            fill_mask()
        out_y()
        ou_s[t, 1] = dot(perm[0], ou_yr[t].reshape(256, 128)).astype(BF16).reshape(8, 32, 128)
        landed = to_positions(ou_s.at[t, 1].reshape(16, 16, 128), yl.at[t], True)
        if t == 0:
            accs_z()
            ah[...] = dot(perm[1], ac_zr[...].reshape(256, 128))
        if last:
            fa_y()
            fa_s[1] = dot(perm[0], fa_yr[...].reshape(256, 128)).astype(BF16).reshape(8, 32, 128)
            fa_z = to_positions(fa_s.at[1].reshape(16, 16, 128), fa_zr, False)

        chunk = {kx: rows_at(lax.rem(x + 4 - kx, 4), 128) for kx in X_ORDER}
        over_sent, over = take(yl.at[t, :, 0:128]), {kx: arrival() for kx in X_ORDER}
        swap_sent, swap = take(bk_cr.at[t]), {kx: arrival() for kx in X_ORDER}

        def forward(kx):
            wait(yl.at[t, pl.ds(0, 128 if kx else 112), pl.ds(0, 128)], landed[kx])
            mine = yl.at[t, chunk[kx], half]
            send(mine, mine, over_sent, over[kx], other_core)

        def compute(kx):
            at = chunk[kx]
            wait(yl.at[t, pl.ds(0, 128), pl.ds(0, 128)], over[kx])
            scores = lax.dot_general(yl[t, at, :], xl[...], NT, preferred_element_type=F32)
            weight = mask[at, :].astype(F32)
            e = (weight * (scores - jnp.where(weight > 2.0, 1.0, 0.0))).astype(BF16)
            err[at, :] = e
            part[t, at, :] = dot(e, xl[...])
            send(part.at[t, at, other_half], bk_cr.at[t, at], swap_sent, swap[kx], other_core)

        if not last:
            back_sent, back_landed = take(bk_zr.at[t, pl.ds(0, 31)]), arrival()
        else:
            cross_sent, cross = take(fin_r), {kx: arrival() for kx in X_ORDER}

        def go_back(kx):
            at = chunk[kx]
            wait(bk_cr.at[t, pl.ds(0, 128)], swap[kx])
            total = (part[t, at, half] + bk_cr[t, at]).astype(BF16)
            if last:
                fin_s[at, :] = total
                send(fin_s.at[at], fin_r.at[at], cross_sent, cross[kx], other_zh)
                return
            hx = lax.rem(x + 4 - kx, 4)
            bk_z[t, pl.ds(hx * 8, 8)] = total.reshape(8, 16, 128)
            for kz in far_z + (0,):
                pz = lax.rem(z + kz, 8)
                if kx == 0 and kz == 0:
                    bk_zr[t, x * 8 + z] = bk_z[t, x * 8 + z]
                else:
                    send(bk_z.at[t, hx * 8 + pz], bk_zr.at[t, x * 8 + z], back_sent, back_landed, dev(hx, y, pz))

        forward(0)
        forward(1)
        compute(0)
        forward(3)
        compute(1)
        go_back(0)
        forward(2)
        compute(3)
        go_back(1)
        compute(2)
        go_back(3)
        go_back(2)

        def users():
            for u in range(4):
                at = pl.ds(u * 256, 256)
                old = xs[at, :]
                grad = lax.dot_general(err[:, u * 256 : u * 256 + 256], yl[t], TN, preferred_element_type=F32)
                grad = grad + SHRINKAGE * old
                acc = ucol[at, :] + jnp.sum(grad * grad, axis=1, keepdims=True) * (1.0 / 256.0)
                ucol[at, :] = acc
                new = old - grad * (rate / jnp.sqrt(acc))
                xs[at, :] = new
                if not last:
                    xl[at, :] = new.astype(BF16)

        users()
        if not last:
            wait(bk_zr.at[t, pl.ds(0, 31)], back_landed)
            bk_s[t] = dot(perm_sum[...], bk_zr[t].reshape(512, 128)).astype(BF16).reshape(8, 32, 128)
            back_y = along_y(bk_s.at[t], bk_yr.at[t])
            sort_words(t + 1)
            fill_mask()
            back_y()
            grad = dot(onehot_t[t], bk_yr[t].reshape(256, 128)) + SHRINKAGE * yh[...]
            acc = ah[...] + grad * grad
            ah[...] = acc
            yh[...] = yh[...] - rate * grad / jnp.sqrt(acc)
        else:
            store = pltpu.make_async_copy(xs, user_out, local_sem.at[len(loads)])
            store.start()
            wait(fa_zr.at[pl.ds(0, 31)], fa_z[0])
            new_sent, new_landed = take(items_new.at[:, 0:128]), arrival()
            for kx in X_ORDER:
                at = chunk[kx]
                wait(fin_r.at[pl.ds(0, 128)], cross[kx])
                old = yl[t, at, half].astype(F32)
                grad = fin_s[at, :].astype(F32) + fin_r[at, :].astype(F32) + SHRINKAGE * old
                before = fa_zr[pl.ds(lax.rem(x + 4 - kx, 4) * 8, 8)].reshape(128, 128).astype(F32)
                items_new[at, half] = old - rate * grad / jnp.sqrt(before + grad * grad)
                mine = items_new.at[at, half]
                send(mine, mine, new_sent, new_landed, other_core)
            wait(items_new.at[:, 0:128], new_landed)
            done = pltpu.make_async_copy(items_new, item_out, local_sem.at[len(loads) + 1])
            done.start()
            for k, ref in enumerate(sends):
                wait(ref, send_sem.at[k])
            store.wait()
            done.wait()


def on_device(
    user_rows, user_accum, item_rows, item_accum, move_lists, tile_lists, tile_counts, rating_bits
):
    smem, anywhere = pl.BlockSpec(memory_space=pltpu.SMEM), pl.BlockSpec(memory_space=pl.ANY)
    v = pltpu.VMEM
    by_y, by_xz = (8, 32, 128), (16, 16, 128)
    new_users, new_items = pl.pallas_call(
        kernel,
        out_shape=(
            jax.ShapeDtypeStruct((1024, 256), F32),
            jax.ShapeDtypeStruct((512, 256), F32),
        ),
        in_specs=[anywhere, anywhere, anywhere, anywhere, anywhere, anywhere, smem, anywhere],
        out_specs=(anywhere, anywhere),
        scratch_shapes=[
            v((1024, 256), F32), v((1024, 256), BF16), v((8, 128), F32), v((1024, 1), F32),
            v((STRATA, 128), jnp.int32), v((STRATA, 1, 1, 32), jnp.int32),
            v((STRATA, 32, 16, 128), jnp.int32), v((512, 256), BF16), v((512, 128), jnp.int32), v((512, 128), F32),
            v((512, 1024), BF16), v((512, 1024), BF16), v((STRATA, 512, 256), BF16), v((STRATA, 512, 256), F32),
            v((256, 128), F32), v((256, 128), F32),
            v((STRATA, 256, 256), BF16), v((2, 256, 256), BF16), v((2, 256, 256), BF16), v((256, 512), BF16),
            v((512, 128), F32), v((512, 128), F32), v((512, 256), F32),
            v((256, 128), BF16), v((2, *by_y), BF16), v(by_y, BF16), v(by_xz, BF16),
            v((256, 128), BF16), v((2, *by_y), BF16), v(by_y, BF16), v(by_xz, BF16),
            v((STRATA, 2, *by_y), BF16), v((STRATA, *by_y), BF16),
            v((2, *by_y), BF16), v(by_y, BF16), v((32, 16, 128), BF16),
            v((STRATA, 512, 128), F32), v((2, 32, 16, 128), BF16), v((2, 32, 16, 128), BF16),
            v((2, *by_y), BF16), v((2, *by_y), BF16),
            v((512, 128), BF16), v((512, 128), BF16),
            pltpu.SemaphoreType.DMA((12,)),
            pltpu.SemaphoreType.DMA((24,)),
            pltpu.SemaphoreType.DMA((64,)),
            pltpu.SemaphoreType.REGULAR,
        ],
        compiler_params=pltpu.CompilerParams(
            collective_id=0, has_side_effects=True, vmem_limit_bytes=60 * 1024 * 1024
        ),
        cost_estimate=pl.CostEstimate(flops=3 * 3 * 2 * 1024 * 512 * 256, bytes_accessed=6 * 1024 * 1024, transcendentals=0),
    )(
        user_rows, user_accum.reshape(8, 128), item_rows, item_accum, move_lists, tile_lists,
        tile_counts.transpose(1, 2, 0).reshape(1, STRATA), rating_bits,
    )
    return new_users, new_items


def solution(mesh):
    in_specs = (
        P(("stratum", "rep"), None),
        P(("stratum", "rep")),
        P("stratum", None),
        P("stratum", None),
        P(),
        P(None, "stratum", "rep", None),
        P(None, "stratum", "rep"),
        P(None, "stratum", "rep", None, None, None),
    )
    out_specs = (P(("stratum", "rep"), None), P("stratum", None))
    return jax.shard_map(
        on_device, mesh=mesh, in_specs=in_specs, out_specs=out_specs, check_vma=False
    )
```

time: 556 us -> 107 us (0.19)
  waiting for transfers between devices: 391 us -> 0 us
  Pallas kernels: 0 us -> 103 us
  starting transfers between devices: 67.8 us -> 0 us
  local copies, waits for them, and re-layouts: 38.7 us -> 3.12 us
  other arithmetic: 21 us -> 0 us
  matrix products: 19.4 us -> 0 us
  between operations: 16.4 us -> 0.65 us
    psum x3 -> x0, waiting for transfers between devices: 237 us -> none  [rep_total(): return lax.psum(item_part, 'rep')]
    all_to_all x6 -> x0, waiting for transfers between devices: 154 us -> none  [the longest x3 84.6 us: on_device(): lax.all_to_all(pieces, 'stratum', split_axis=1, concat_axis=1, tiled=True)]
    pallas_call x0 -> x1, Pallas kernels: none -> 103 us  [on_device(): pl.pallas_call(kernel, out_shape=(jax.ShapeDtypeStruct((1024, 256), F32),...]
    all_to_all x6 -> x0, starting transfers between devices: 67.7 us -> none  [the longest x3 42.2 us: on_device(): lax.all_to_all(pieces, 'stratum', split_axis=1, concat_axis=1, tiled=True)]
    dot_general x25 -> x0, matrix products: 19.4 us -> none  [the longest x5 7.12 us: one_group(): jnp.einsum('gc,gir->cir', col_hot, item_part, precision=lax.Precision.HIG...]
    gather x23 -> x0, local copies, waits for them, and re-layouts: 18.2 us -> none  [the longest x5 5.61 us: one_group(): observed = unpack_bits(jnp.take(bit_words, clamped, axis=0))]
    convert_element_type x8 -> x0, other arithmetic: 6.07 us -> none  [the longest x5 3.43 us: one_group(): active = (position < tile_count).astype(jnp.float32)]
    slice x7 -> x0, local copies, waits for them, and re-layouts: 5.97 us -> none  [the longest x5 3.92 us: on_device(): item_low = item_state[0].astype(jnp.bfloat16)]
  transfers between devices with their start and end apart: 9 -> 0, of which waited for: 9 -> 0; matrix products, arithmetic and copies ran while one was open for 2% -> 0% of each run, Pallas kernels for 0% -> 0%
where the time goes in v2:
time: 107 us
  Pallas kernels  103 us (96%)
  local copies, waits for them, and re-layouts  3.12 us (3%)
    pallas_call x1, Pallas kernels, on_device(): pl.pallas_call(kernel, out_shape=(jax.ShapeDtypeStruct((1024, 256), F32),...  103 us
    unnamed x4, local copies, waits for them, and re-layouts  3.12 us

profile of v2, /device:TPU:1, one launch (start us, length us, event | category | flops | bytes accessed | tf_op | source)
XLA Modules:
  0.0 107.1 jit_solution(8631923475222098796)
XLA Ops:
  0.6 103.3 %shard_map.95 = (f32[1024,256]{1,0:T(8,128)}, f32[512,256]{1,0:T(8,128)}) custom-call(f32[1024,256]{1,0:T(8,128)} %user_hbm.1, f32[8,128]{1,0:T(8,128)} %bitcast.2, f32[512,256]{1,0:T(8,128)} %item_hbm.1, f32[512,256]{1,0:T(8,128)} %iacc_hbm.1, s32[3,128]{1,0:T(4,128)} %move_hbm.1, s32[3,1,1,32]{3,2,1,0:T(1,128)} %list_hbm.1, s32[1,3]{1,0:T(1,128)} %bitcast.3, ...), custom_call_target="tpu_custom_call" | custom-call | flops 2415919104 | bytes 6291456 | tf_op jit(solution)/shard_map/pallas_call | solution.py:374
  104.0 0.0 copy-start
  104.0 2.3 %copy.12 = f32[1024,256]{1,0:T(8,128)} copy(f32[1024,256]{1,0:T(8,128)} %get-tuple-element.4) | data formatting | bytes 2097152
  106.3 0.0 copy-done
  106.3 0.8 copy.13
Async XLA Ops:
  104.0 2.3 %copy-start = (f32[512,256]{1,0:T(8,128)S(1)}, f32[512,256]{1,0:T(8,128)}, u32[]{:S(2)}) copy-start(f32[512,256]{1,0:T(8,128)} %get-tuple-element.5) | copy-start | bytes 1572868
